TPU v7x, 128 devices: a whole 4x4x4 slice. The times are simulated.
128 devices in a mesh: row: 8 (over y_lo, x), col: 16 (over z, y_hi, core).
Axes of the slice: x: 4, y: 4 (y_hi: 2, y_lo: 2; y = y_hi * 2 + y_lo), z: 4, core: 2. Of those that a mesh axis runs over, the one named last changes fastest.
Arguments:
- pair_products: bfloat16 [2, 46080, 512], P(None, 'row', 'col'), may hold values from -6 to 6
- eigvecs: bfloat16 [46080, 4608], P('row', 'col'), may hold values from -0.02734375 to 0.02734375
- valence_band: int32 [2, 64], replicated, may hold values from 0 to 5483
- cond_band: int32 [2, 8], replicated, may hold values from 0 to 4095
- valence_energy: float32 [5484], replicated, may hold values from -15 to -0.5
- cond_energy: float32 [4096], replicated, may hold values from 0.5 to 20
Outputs:
- chi: float32 [12, 4608, 4608], P(None, 'row', 'col')
All inputs are finite; a program needn't handle non-finite values.
Results may differ from a plain program's by a relative error of at most 0.0045.
Values may be sent and summed in bfloat16 or wider, within the bound.
A program may use at most 64 MiB of HBM per device.

v0:
```python
import jax
import jax.numpy as jnp
from jax import lax
from jax.sharding import PartitionSpec as P

NFREQ = 12


def pair_factor(valence_band, cond_band, valence_energy, cond_energy):
    nblk = valence_band.shape[0]
    nval = valence_energy.shape[0]
    ncon = cond_energy.shape[0]
    val_hot = (valence_band[:, :, None] == jnp.arange(nval, dtype=jnp.int32)[None, None, :]).astype(
        jnp.float32
    )
    con_hot = (cond_band[:, :, None] == jnp.arange(ncon, dtype=jnp.int32)[None, None, :]).astype(
        jnp.float32
    )
    low = jnp.sum(val_hot * valence_energy[None, None, :], axis=2)
    high = jnp.sum(con_hot * cond_energy[None, None, :], axis=2)
    delta = (high[:, None, :] - low[:, :, None]).reshape(nblk, -1)
    omega = 1.5 * jnp.arange(NFREQ).astype(jnp.float32)
    scale = 1.0 / jnp.sqrt(jnp.float32(delta.shape[0] * delta.shape[1]))
    return -4.0 * delta[:, None, :] / (delta[:, None, :] ** 2 + omega[None, :, None] ** 2) * scale


def local(pair_products, eigvecs, valence_band, cond_band, valence_energy, cond_energy):
    nrow = lax.axis_size("row")
    ncol = lax.axis_size("col")
    s_col = eigvecs.shape[1]
    total_s = s_col * ncol
    s_row = total_s // nrow
    factor = pair_factor(valence_band, cond_band, valence_energy, cond_energy)
    chi = jnp.zeros((NFREQ, s_row, s_col), jnp.float32)
    for blk in range(pair_products.shape[0]):
        partial_value = lax.dot_general(
            eigvecs,
            lax.all_gather(pair_products[blk], "col", axis=1, tiled=True),
            (((0,), (0,)), ((), ())),
            preferred_element_type=jnp.float32,
        )
        summed = lax.psum(partial_value, "row")
        full = lax.all_gather(summed.astype(jnp.bfloat16), "col", axis=0, tiled=True)
        own_cols = lax.dynamic_slice_in_dim(full, lax.axis_index("col") * s_col, s_col, 0)
        own_rows = lax.dynamic_slice_in_dim(full, lax.axis_index("row") * s_row, s_row, 0)
        scaled = (own_rows[None, :, :].astype(jnp.float32) * factor[blk][:, None, :]).astype(
            jnp.bfloat16
        )
        chi = chi + jnp.einsum("wsp,tp->wst", scaled, own_cols, preferred_element_type=jnp.float32)
    return chi


def solution(mesh):
    return jax.shard_map(
        local,
        mesh=mesh,
        in_specs=(P(None, "row", "col"), P("row", "col"), P(), P(), P(), P()),
        out_specs=P(None, "row", "col"),
        check_vma=False,
    )
```

profile of v0, /device:TPU:9, one launch (start us, length us, event | category | flops | bytes accessed | tf_op | source)
XLA Modules:
  0.0 340.3 jit_solution(11251181033512500666)
XLA Ops:
  6.5 0.0 copy-start
  6.5 0.0 all-gather.11.cloned.1.call-start
  6.5 2.2 fusion.17
  8.7 0.0 all-gather.11.cloned.1.call-update
  8.7 0.0 all-gather.13.cloned.1.call-start
  8.8 0.7 all-gather.13.cloned.1.call-update
  9.5 0.0 all-gather.7.cloned.1.call-start
  9.5 64.8 %all-gather.11.cloned.1.call-done = bf16[1,5760,512]{1,2,0:T(8,128)(2,1)} async-done(((bf16[1,5760,32]{1,2,0:T(8,128)(2,1)}), bf16[1,5760,512]{1,2,0:T(8,128)(2,1)}) %all-gather.11.cloned.1.call-update) | async-done | bytes 5898256 | tf_op jit(solution)/shard_map/all_gather | solution.py:38
  74.3 0.0 copy-done
  74.3 5.4 %fusion.8 = f32[288,512]{1,0:T(8,128)} fusion(bf16[5760,288]{0,1:T(8,128)(2,1)S(1)} %copy-done, bf16[1,5760,512]{1,2,0:T(8,128)(2,1)} %all-gather.11.cloned.1.call-done), kind=kOutput, calls=%fused_computation.10 | convolution fusion | flops 1698693120 | bytes 9805824 | tf_op jit(solution)/shard_map/dot_general | solution.py:36
  79.7 0.0 copy-start.2
  79.7 0.0 copy-start.3
  79.7 0.0 copy-start.1
  79.7 0.0 copy-start.4
  79.7 57.3 %all-gather.13.cloned.1.call-done = bf16[1,5760,512]{1,2,0:T(8,128)(2,1)} async-done(((bf16[1,5760,32]{1,2,0:T(8,128)(2,1)}), bf16[1,5760,512]{1,2,0:T(8,128)(2,1)}) %all-gather.13.cloned.1.call-update) | async-done | bytes 5898256 | tf_op jit(solution)/shard_map/all_gather | solution.py:38
  137.1 5.4 %fusion.6 = f32[288,512]{1,0:T(8,128)} fusion(bf16[5760,288]{0,1:T(8,128)(2,1)S(1)} %copy-done, bf16[1,5760,512]{1,2,0:T(8,128)(2,1)} %all-gather.13.cloned.1.call-done), kind=kOutput, calls=%fused_computation.8 | convolution fusion | flops 1698693120 | bytes 9805824 | tf_op jit(solution)/shard_map/dot_general | solution.py:36
  142.5 57.1 %all-reduce.2 = (bf16[288,512]{1,0:T(8,128)(2,1)}, bf16[288,512]{1,0:T(8,128)(2,1)}) all-reduce(f32[288,512]{1,0:T(8,128)} %fusion.8, f32[288,512]{1,0:T(8,128)} %fusion.6), channel_id=1, replica_groups=mesh['row'=8,'col'=16] {'row'}, use_global_device_ids=true, to_apply=%region_0.0 | all-reduce | flops 294912 | bytes 1769472 | tf_op jit(solution)/shard_map/psum | solution.py:42
  199.6 0.0 all-gather.7.cloned.1.call-update
  199.7 0.0 all-gather.9.cloned.1.call-start
  199.7 0.5 all-gather.9.cloned.1.call-update
  200.3 0.0 copy-done.2
  200.3 0.0 copy-done.3
  200.3 0.2 select_reduce_fusion.1
  200.5 0.0 copy-done.1
  200.5 0.0 copy-done.4
  200.5 0.5 select_reduce_fusion
  201.0 0.1 subtract_multiply_fusion.1
  201.1 0.1 integer_pow.20
  201.2 0.1 mul.89
  201.3 0.1 divide_multiply_fusion
  201.4 63.4 %all-gather.7.cloned.1.call-done = bf16[4608,512]{1,0:T(8,128)(2,1)} async-done(((bf16[288,512]{1,0:T(8,128)(2,1)}), bf16[4608,512]{1,0:T(8,128)(2,1)}) %all-gather.7.cloned.1.call-update) | async-done | bytes 4718608 | tf_op jit(solution)/shard_map/all_gather | solution.py:43
  264.8 2.2 dynamic-slice_convert_fusion.1
  267.1 55.5 %all-gather.9.cloned.1.call-done = bf16[4608,512]{1,0:T(8,128)(2,1)} async-done(((bf16[288,512]{1,0:T(8,128)(2,1)}), bf16[4608,512]{1,0:T(8,128)(2,1)}) %all-gather.9.cloned.1.call-update) | async-done | bytes 4718608 | tf_op jit(solution)/shard_map/all_gather | solution.py:43
  322.6 1.2 dynamic-slice_convert_fusion
  323.8 3.8 %fusion = f32[12,576,288]{1,2,0:T(8,128)S(1)} fusion(f32[12,512]{1,0:T(8,128)S(1)} %get-tuple-element.10, f32[576,512]{1,0:T(8,128)} %dynamic-slice_convert_fusion.1, bf16[4608,512]{1,0:T(8,128)(2,1)} %all-gather.7.cloned.1.call-done, s32[]{:T(128)S(6)} %select_n.9), kind=kOutput, calls=%fused_computation.2 | convolution fusion | flops 2045509632 | bytes 9461764 | tf_op jit(solution)/shard_map/wsp,tp->wst/dot_general | solution.py:49
  327.7 6.1 %fusion.10 = f32[12,576,288]{1,2,0:T(8,128)} fusion(f32[12,576,288]{1,2,0:T(8,128)S(1)} %fusion, f32[12,512]{1,0:T(8,128)S(1)} %get-tuple-element.9, f32[576,512]{1,0:T(8,128)S(1)} %dynamic-slice_convert_fusion, bf16[4608,512]{1,0:T(8,128)(2,1)} %all-gather.9.cloned.1.call-done, s32[]{:T(128)S(6)} %select_n.9), kind=kOutput, calls=%fused_computation.12 | convolution fusion | flops 2047500288 | bytes 17424388 | tf_op jit(solution)/shard_map/wsp,tp->wst/dot_general | solution.py:49
  (2 shorter events, 0.0 us)
Async XLA Ops:
  6.5 67.7 %copy-start = (bf16[5760,288]{0,1:T(8,128)(2,1)S(1)}, bf16[5760,288]{0,1:T(8,128)(2,1)}, u32[]{:S(2)}) copy-start(bf16[5760,288]{0,1:T(8,128)(2,1)} %param.7) | copy-start | bytes 9953284
  6.5 67.7 %all-gather.11.cloned.1.call-start = ((), (), s32[]{:S(2)}) async-start(), calls=%async_computation.2 | async-start | bytes 6266880 | tf_op jit(solution)/shard_map/all_gather | solution.py:38
  8.7 128.3 %all-gather.13.cloned.1.call-start = ((), (), s32[]{:S(2)}) async-start(), calls=%async_computation.3 | async-start | bytes 6266880 | tf_op jit(solution)/shard_map/all_gather | solution.py:38
  9.5 255.4 %all-gather.7.cloned.1.call-start = ((), (), s32[]{:S(2)}) async-start(), calls=%async_computation | async-start | bytes 5013504 | tf_op jit(solution)/shard_map/all_gather | solution.py:43
  79.7 120.5 %copy-start.2 = (f32[4096]{0:T(1024)S(1)}, f32[4096]{0:T(1024)}, u32[]{:S(2)}) copy-start(f32[4096]{0:T(1024)} %param.11) | copy-start | bytes 49156
  79.7 120.6 %copy-start.3 = (s32[2,8]{1,0:T(2,128)S(1)}, s32[2,8]{1,0:T(2,128)}, u32[]{:S(2)}) copy-start(s32[2,8]{1,0:T(2,128)} %param.9) | copy-start | bytes 196
  79.7 120.8 %copy-start.1 = (f32[5484]{0:T(1024)S(1)}, f32[5484]{0:T(1024)}, u32[]{:S(2)}) copy-start(f32[5484]{0:T(1024)} %param.10) | copy-start | bytes 65812
  79.7 120.8 %copy-start.4 = (s32[2,64]{1,0:T(2,128)S(1)}, s32[2,64]{1,0:T(2,128)}, u32[]{:S(2)}) copy-start(s32[2,64]{1,0:T(2,128)} %param.8) | copy-start | bytes 1540
  199.7 123.0 %all-gather.9.cloned.1.call-start = ((), (), s32[]{:S(2)}) async-start(), calls=%async_computation.1 | async-start | bytes 5013504 | tf_op jit(solution)/shard_map/all_gather | solution.py:43
Sparse Core Ops, SparseCore 0:
  9.8 64.4 all-gather.10
  76.7 60.2 all-gather.12
  199.8 65.0 all-gather.6
  267.2 55.4 all-gather.8
where the time goes:
time: 343 us; the launch traced here: 340 us
  waiting for transfers between devices  242 us (71%)
  blocking collectives  57.1 us (17%)
  matrix products  20.8 us (6%)
  between operations  13.2 us (4%)
  other arithmetic  4.33 us (1%)
    all_gather x2, waiting for transfers between devices, local(): lax.all_gather(pair_products[blk], 'col', axis=1, tiled=True)  122 us
    all_gather x2, waiting for transfers between devices, local(): lax.all_gather(summed.astype(jnp.bfloat16), 'col', axis=0, tiled=True)  119 us
    psum x1, blocking collectives, local(): summed = lax.psum(partial_value, 'row')  57.1 us
    dot_general x2, matrix products, local(): lax.dot_general(eigvecs, lax.all_gather(pair_products[blk], 'col', axis=1...  10.9 us
    dot_general x2, matrix products, local(): jnp.einsum('wsp,tp->wst', scaled, own_cols, preferred_element_type=jnp.fl...  9.95 us
  transfers between devices with their start and end apart: 4, of which 4 were waited for; matrix products, arithmetic and copies ran while one was open for 3% of the time, Pallas kernels for 0%

commit v1 on v0

v1 whole, which is shorter than its diff:
```python
import jax
import jax.numpy as jnp
from jax import lax
from jax.experimental import pallas as pl
from jax.experimental.pallas import tpu as pltpu
from jax.sharding import PartitionSpec as P

NFREQ = 12
MESH = pl.DeviceIdType.MESH
LANE = 128
TA1, TA2, TB1, TB2 = 13, 13, 10, 9
SLICE = 16


def pair_factor(valence_band, cond_band, valence_energy, cond_energy):
    nblk = valence_band.shape[0]
    nval = valence_energy.shape[0]
    ncon = cond_energy.shape[0]
    val_hot = valence_band[:, :, None] == jnp.arange(nval, dtype=jnp.int32)[None, None, :]
    con_hot = cond_band[:, :, None] == jnp.arange(ncon, dtype=jnp.int32)[None, None, :]
    low = jnp.sum(jnp.where(val_hot, valence_energy[None, None, :], 0.0), axis=2)
    high = jnp.sum(jnp.where(con_hot, cond_energy[None, None, :], 0.0), axis=2)
    low = low.reshape(nblk, 8, 2, 4).transpose(2, 1, 0, 3)
    delta = (high[None, None, :, None, :] - low[:, :, :, :, None]).reshape(1, -1)
    omega = 1.5 * jnp.arange(NFREQ).astype(jnp.float32)
    scale = 1.0 / jnp.sqrt(jnp.float32(delta.shape[1]))
    return -4.0 * delta / (delta**2 + omega[:, None] ** 2) * scale


def project_kernel(p_hbm, e_hbm, rows_out, cols_out, pairs, eig, total, landed, halves, spread,
                   gather_send, gather_recv, copy_sem, eig_send, eig_recv, sum_send, sum_recv,
                   spread_send, spread_recv, cols_send, cols_recv, rows_send, rows_recv, local_sem):
    row, col = lax.axis_index("row"), lax.axis_index("col")
    core = lax.rem(col, 2)
    j = col // 2
    z, h = j // 2, lax.rem(j, 2)
    ylo = row // 4
    m_half = e_hbm.shape[0]
    m_all = 2 * m_half

    def seat(zz, hh, cc):
        return (row, zz * 4 + hh * 2 + cc)

    up = seat(lax.rem(z + 1, 4), h, core)
    down = seat(lax.rem(z + 3, 4), h, core)
    across = seat(z, 1 - h, core)
    twin = (row, col + 1 - 2 * core)

    block_rows = p_hbm.shape[1]
    local = [
        pltpu.make_async_copy(p_hbm.at[b], pairs.at[pl.ds(b * block_rows, block_rows)], copy_sem.at[b])
        for b in range(2)
    ]
    mine = pl.ds(pl.multiple_of(core * m_half, 16), m_half)
    local.append(pltpu.make_async_copy(e_hbm, eig.at[mine], copy_sem.at[2]))
    for c in local:
        c.start()

    barrier = pltpu.get_barrier_semaphore()

    def greet_rows(d, carry):
        other = lax.rem(row + d, 8)
        for c in range(2):
            pl.semaphore_signal(barrier, inc=1, device_id=(other, j * 2 + c), device_id_type=MESH)
        return carry

    def greet_cols(d, carry):
        other = lax.rem(j + d, 8)
        pl.semaphore_signal(barrier, inc=1, device_id=(row, other * 2 + core), device_id_type=MESH)
        return carry

    lax.fori_loop(1, 8, greet_rows, 0)
    lax.fori_loop(1, 8, greet_cols, 0)
    pl.semaphore_signal(barrier, inc=1, device_id=twin, device_id_type=MESH)
    pl.semaphore_wait(barrier, 22)

    eig_copy = pltpu.make_async_remote_copy(
        e_hbm, eig.at[mine], eig_send, eig_recv, device_id=twin, device_id_type=MESH
    )

    a0, a1, a2 = 0, TA1 * LANE, (TA1 + TA2) * LANE
    b1, b2 = a2 + TB1 * LANE, a2 + (TB1 + TB2) * LANE
    piece = {"A": (a0, a2), "A1": (a0, a1), "A2": (a1, a2), "B": (a2, b2), "B1": (a2, b1), "B2": (b1, b2)}

    slot_of = {(0, 0): 0, (0, 1): 1, (1, 0): 2, (3, 0): 3, (1, 1): 4, (3, 1): 5, (2, 0): 6, (2, 1): 7}
    place_of = {s: k for k, s in slot_of.items()}
    copies = {}

    def region(slot, name):
        lo, hi = piece[name]
        return pairs.at[pl.ds(64 * slot, 64), pl.ds(lo, hi - lo)]

    def send(slot, name, way):
        dz, dh = place_of[slot]
        target, there = {
            "up": (up, ((dz + 3) % 4, dh)),
            "down": (down, ((dz + 1) % 4, dh)),
            "across": (across, (dz, 1 - dh)),
        }[way]
        there = slot_of[there]
        n = len(copies)
        c = pltpu.make_async_remote_copy(
            region(slot, name), region(there, name), gather_send.at[n], gather_recv.at[n],
            device_id=target, device_id_type=MESH,
        )
        copies[(there, name)] = c
        c.start()

    def arrive(slot, name):
        copies[(slot, name)].wait_recv()

    def multiply(g, name):
        lo, hi = piece[name]
        rows = pl.ds(128 * g, 128)
        value = lax.dot_general(
            pairs[rows, lo:hi], eig[:, lo:hi], (((1,), (1,)), ((), ())), preferred_element_type=jnp.float32
        )
        if name == "B":
            total[rows, :] = value
        else:
            total[rows, :] += value

    def pair_row(g, owner, jj, cc):
        yo = owner // 4
        if g == 0:
            dz, dh = 0, yo
        elif g == 3:
            dz, dh = 2, yo
        else:
            dz, dh = 1 + 2 * yo, g - 1
        zz = lax.rem(jj // 2 + dz, 4)
        hh = lax.rem(lax.rem(jj, 2) + dh, 2)
        return pl.multiple_of(cc * 512 + (zz * 2 + hh) * 64 + lax.rem(owner, 4) * SLICE, SLICE)

    def sum_start(g):
        def go(d, carry):
            to = lax.rem(row + d, 8)
            pltpu.make_async_remote_copy(
                total.at[pl.ds(pl.multiple_of(128 * g + to * SLICE, SLICE), SLICE)],
                landed.at[g, pl.ds(pl.multiple_of((d - 1) * SLICE, SLICE), SLICE)],
                sum_send.at[g], sum_recv.at[g],
                device_id=(to, col), device_id_type=MESH,
            ).start()
            return carry

        lax.fori_loop(1, 8, go, 0)

    def sum_end(g):
        seven = landed.at[g]
        pltpu.make_async_copy(seven, seven, sum_recv.at[g]).wait()
        value = total[pl.ds(pl.multiple_of(128 * g + row * SLICE, SLICE), SLICE), :]
        for d in range(7):
            value = value + landed[g, d * SLICE:(d + 1) * SLICE, :]
        value = value.astype(spread.dtype)
        spread[g, 0] = value
        halves[g, 0] = value[:, :m_half]
        halves[g, 1] = value[:, m_half:]

        def go(d, carry):
            to = lax.rem(j + d, 8)
            pltpu.make_async_remote_copy(
                spread.at[g, 0], spread.at[g, d], spread_send.at[g], spread_recv.at[g],
                device_id=(row, to * 2 + core), device_id_type=MESH,
            ).start()
            return carry

        lax.fori_loop(1, 8, go, 0)
        first = pair_row(g, row, j, core)

        def go_cols(d, carry):
            to = lax.rem(row + d, 8)
            for c in range(2):
                pltpu.make_async_remote_copy(
                    halves.at[g, c], cols_out.at[pl.ds(first, SLICE)], cols_send, cols_recv,
                    device_id=(to, j * 2 + c), device_id_type=MESH,
                ).start()
            return carry

        lax.fori_loop(1, 8, go_cols, 0)
        pltpu.make_async_remote_copy(
            halves.at[g, 1 - core], cols_out.at[pl.ds(first, SLICE)], cols_send, cols_recv,
            device_id=twin, device_id_type=MESH,
        ).start()
        pltpu.make_async_copy(halves.at[g, core], cols_out.at[pl.ds(first, SLICE)], local_sem.at[g]).start()

    def deal(g):
        seven = spread.at[g, pl.ds(1, 7)]
        pltpu.make_async_copy(seven, seven, spread_recv.at[g]).wait()

        def go(d, carry):
            to = lax.rem(row + d, 8)
            first = pair_row(g, row, to, core)
            for c in range(2):
                pltpu.make_async_remote_copy(
                    spread.at[g, lax.rem(j + 8 - to, 8)], rows_out.at[pl.ds(first, SLICE)], rows_send, rows_recv,
                    device_id=(to, j * 2 + c), device_id_type=MESH,
                ).start()
            return carry

        lax.fori_loop(1, 8, go, 0)
        first = pair_row(g, row, row, core)
        kept = spread.at[g, lax.rem(j + 8 - row, 8)]
        pltpu.make_async_remote_copy(
            kept, rows_out.at[pl.ds(first, SLICE)], rows_send, rows_recv, device_id=twin, device_id_type=MESH
        ).start()
        pltpu.make_async_copy(kept, rows_out.at[pl.ds(first, SLICE)], local_sem.at[4 + g]).start()

    local[0].wait()
    local[1].wait()
    send(0, "B", "up")
    send(0, "B", "down")
    send(0, "A", "across")
    eig_copy.start()
    arrive(3, "B")
    send(0, "A", "up")
    send(3, "B1", "up")
    arrive(2, "B")
    send(0, "A", "down")
    send(2, "B2", "down")
    send(0, "B", "across")
    arrive(1, "A")
    send(3, "B", "across")
    local[2].wait()
    eig_copy.wait()
    arrive(1, "B")
    send(2, "B", "across")
    multiply(0, "B")
    arrive(6, "B1")
    arrive(6, "B2")
    send(6, "B1", "across")
    send(6, "B2", "across")
    multiply(0, "A1")
    arrive(3, "A")
    send(1, "A", "up")
    send(3, "A1", "up")
    arrive(2, "A")
    send(1, "A", "down")
    send(2, "A2", "down")
    multiply(0, "A2")
    sum_start(0)
    multiply(1, "B")
    multiply(1, "A1")
    multiply(1, "A2")
    sum_start(1)
    sum_end(0)
    arrive(5, "B")
    arrive(4, "B")
    multiply(2, "B")
    sum_end(1)
    deal(0)
    arrive(5, "A")
    send(5, "A1", "up")
    arrive(4, "A")
    send(4, "A2", "down")
    multiply(2, "A1")
    multiply(2, "A2")
    sum_start(2)
    deal(1)
    arrive(7, "B1")
    arrive(7, "B2")
    multiply(3, "B")
    sum_end(2)
    arrive(6, "A1")
    arrive(7, "A1")
    multiply(3, "A1")
    arrive(6, "A2")
    arrive(7, "A2")
    multiply(3, "A2")
    sum_start(3)
    deal(2)
    sum_end(3)
    deal(3)

    for c in copies.values():
        c.wait_send()
    for g in range(4):
        seven = landed.at[g]
        pltpu.make_async_copy(seven, seven, sum_send.at[g]).wait()
        seven = spread.at[g, pl.ds(1, 7)]
        pltpu.make_async_copy(seven, seven, spread_send.at[g]).wait()
        pltpu.make_async_copy(halves.at[g, 0], cols_out.at[pl.ds(0, SLICE)], local_sem.at[g]).wait()
        pltpu.make_async_copy(spread.at[g, 0], rows_out.at[pl.ds(0, SLICE)], local_sem.at[4 + g]).wait()
    many = pl.ds(0, 60 * SLICE)
    for ref, s in ((cols_out, cols_send), (cols_out, cols_recv), (rows_out, rows_send), (rows_out, rows_recv)):
        pltpu.make_async_copy(ref.at[many], ref.at[many], s).wait()


def project(pairs_t, eig_t):
    nblk, pair_rows, depth = pairs_t.shape
    m_half = eig_t.shape[0]
    m_all = 2 * m_half
    bf16, f32 = jnp.bfloat16, jnp.float32
    dma = pltpu.SemaphoreType.DMA
    return pl.pallas_call(
        project_kernel,
        out_shape=(
            jax.ShapeDtypeStruct((1024, m_all), bf16),
            jax.ShapeDtypeStruct((1024, m_half), bf16),
        ),
        in_specs=[pl.BlockSpec(memory_space=pl.ANY)] * 2,
        out_specs=(pl.BlockSpec(memory_space=pl.ANY),) * 2,
        scratch_shapes=[
            pltpu.VMEM((512, depth), bf16),
            pltpu.VMEM((m_all, depth), bf16),
            pltpu.VMEM((512, m_all), f32),
            pltpu.VMEM((4, 7 * SLICE, m_all), f32),
            pltpu.VMEM((4, 2, SLICE, m_half), bf16),
            pltpu.VMEM((4, 8, SLICE, m_all), bf16),
            dma((18,)), dma((18,)), dma((3,)), dma, dma, dma((4,)), dma((4,)),
            dma((4,)), dma((4,)), dma, dma, dma, dma, dma((8,)),
        ],
        compiler_params=pltpu.CompilerParams(
            collective_id=0, has_side_effects=True, vmem_limit_bytes=48 * 2**20
        ),
        name="project",
    )(pairs_t, eig_t)


def chi_kernel(factor_ref, rows_ref, cols_ref, out_ref, cols_t):
    @pl.when(pl.program_id(0) == 0)
    def _():
        cols_t[...] = cols_ref[...].astype(jnp.float32).T

    scaled = (cols_t[...] * factor_ref[pl.ds(pl.program_id(0), 1), :]).astype(jnp.bfloat16)
    out_ref[0] = jnp.dot(scaled, rows_ref[...], preferred_element_type=jnp.float32)


def polarizability(factor, rows, cols):
    n, s_rows = rows.shape
    s_cols = cols.shape[1]
    return pl.pallas_call(
        chi_kernel,
        grid=(NFREQ,),
        out_shape=jax.ShapeDtypeStruct((NFREQ, s_cols, s_rows), jnp.float32),
        in_specs=[
            pl.BlockSpec((NFREQ, n), lambda w: (0, 0)),
            pl.BlockSpec((n, s_rows), lambda w: (0, 0)),
            pl.BlockSpec((n, s_cols), lambda w: (0, 0)),
        ],
        out_specs=pl.BlockSpec((1, s_cols, s_rows), lambda w: (w, 0, 0)),
        scratch_shapes=[pltpu.VMEM((s_cols, n), jnp.float32)],
        compiler_params=pltpu.CompilerParams(vmem_limit_bytes=32 * 2**20),
        name="chi",
    )(factor, rows, cols)


def local(pair_products, eigvecs, valence_band, cond_band, valence_energy, cond_energy):
    factor = pair_factor(valence_band, cond_band, valence_energy, cond_energy)
    rows, cols = project(pair_products.transpose(0, 2, 1), eigvecs.T)
    return polarizability(factor, rows, cols).transpose(0, 2, 1)


def solution(mesh):
    return jax.shard_map(
        local,
        mesh=mesh,
        in_specs=(P(None, "row", "col"), P("row", "col"), P(), P(), P(), P()),
        out_specs=P(None, "row", "col"),
        check_vma=False,
    )
```

time: 343 us -> 113 us (0.33)
  waiting for transfers between devices: 242 us -> 0 us
  Pallas kernels: 0 us -> 105 us
  blocking collectives: 57.1 us -> 0 us
  matrix products: 20.8 us -> 0 us
  between operations: 13.2 us -> 0.05 us
    all_gather x4 -> x0, waiting for transfers between devices: 241 us -> none  [the longest x2 122 us: local(): lax.all_gather(pair_products[blk], 'col', axis=1, tiled=True)]
    pallas_call x0 -> x2, Pallas kernels: none -> 105 us  [the longest x1 95.2 us: project(): pl.pallas_call(project_kernel, out_shape=(jax.ShapeDtypeStruct((1024, m_a...]
    psum x1 -> x0, blocking collectives: 57.1 us -> none  [local(): summed = lax.psum(partial_value, 'row')]
    dot_general x4 -> x0, matrix products: 20.8 us -> none  [the longest x2 10.9 us: local(): lax.dot_general(eigvecs, lax.all_gather(pair_products[blk], 'col', axis=1...]
  transfers between devices with their start and end apart: 4 -> 0, of which waited for: 4 -> 0; matrix products, arithmetic and copies ran while one was open for 3% -> 0% of each run, Pallas kernels for 0% -> 0%
where the time goes in v1:
time: 113 us; the launch traced here: 111 us
  Pallas kernels  105 us (93%)
  local copies, waits for them, and re-layouts  3.37 us (3%)
  other arithmetic  2.37 us (2%)
    pallas_call x1, Pallas kernels, project(): pl.pallas_call(project_kernel, out_shape=(jax.ShapeDtypeStruct((1024, m_a...  95.2 us
    pallas_call x1, Pallas kernels, polarizability(): pl.pallas_call(chi_kernel, grid=(NFREQ,), out_shape=jax.ShapeDtypeStruct(...  10 us
    unnamed x4, local copies, waits for them, and re-layouts  3.05 us

profile of v1, /device:TPU:9, one launch (start us, length us, event | category | flops | bytes accessed | tf_op | source)
XLA Modules:
  0.0 111.0 jit_solution(8506495952379814828)
XLA Ops:
  0.0 1.3 %select_reduce_fusion = f32[2,64]{1,0:T(2,128)S(1)} fusion(f32[5484]{0:T(1024)} %param.10, s32[2,64]{1,0:T(2,128)} %param.8), kind=kLoop, calls=%fused_computation | loop fusion | flops 2105728 | bytes 22960 | tf_op jit(solution)/shard_map/reduce_sum | solution.py:21
  1.3 0.9 select_reduce_fusion.1
  2.2 0.1 reshape.46
  2.3 0.1 subtract_multiply_fusion.1
  2.4 0.1 mul.29
  2.5 0.1 integer_pow.20
  2.6 0.1 divide_multiply_fusion.factor_ref
  2.7 0.0 copy-start
  2.7 1.9 %copy-done = bf16[5760,288]{0,1:T(8,128)(2,1)S(1)} copy-done((bf16[5760,288]{0,1:T(8,128)(2,1)S(1)}, bf16[5760,288]{0,1:T(8,128)(2,1)}, u32[]{:S(2)}) %copy-start) | copy-done | bytes 3317784
  4.7 0.0 copy-start.1
  4.7 1.1 %copy-done.1 = bf16[2,5760,32]{1,2,0:T(8,128)(2,1)S(1)} copy-done((bf16[2,5760,32]{1,2,0:T(8,128)(2,1)S(1)}, bf16[2,5760,32]{1,2,0:T(8,128)(2,1)}, u32[]{:S(2)}) %copy-start.1) | copy-done | bytes 737304
  5.8 95.2 %project.1 = (bf16[1024,576]{1,0:T(8,128)(2,1)S(1)}, bf16[1024,288]{1,0:T(8,128)(2,1)S(1)}) custom-call(bf16[2,32,5760]{2,1,0:T(8,128)(2,1)S(1)} %bitcast.5, bf16[288,5760]{1,0:T(8,128)(2,1)S(1)} %bitcast.4), custom_call_target="tpu_custom_call" | custom-call | tf_op jit(solution)/shard_map/project/pallas_call | solution.py:294
  101.0 10.0 %chi.1 = f32[12,288,576]{2,1,0:T(8,128)} custom-call(f32[12,1024]{1,0:T(8,128)S(1)} %divide_multiply_fusion.factor_ref, bf16[1024,576]{1,0:T(8,128)(2,1)S(1)} %get-tuple-element.7.rows_ref, bf16[1024,288]{1,0:T(8,128)(2,1)S(1)} %get-tuple-element.8.cols_ref), custom_call_target="tpu_custom_call" | custom-call | tf_op jit(solution)/shard_map/chi/pallas_call | solution.py:331
  (2 shorter events, 0.0 us)
Async XLA Ops:
  2.7 1.9 %copy-start = (bf16[5760,288]{0,1:T(8,128)(2,1)S(1)}, bf16[5760,288]{0,1:T(8,128)(2,1)}, u32[]{:S(2)}) copy-start(bf16[5760,288]{0,1:T(8,128)(2,1)} %param.7) | copy-start | bytes 9953284
  4.7 1.1 %copy-start.1 = (bf16[2,5760,32]{1,2,0:T(8,128)(2,1)S(1)}, bf16[2,5760,32]{1,2,0:T(8,128)(2,1)}, u32[]{:S(2)}) copy-start(bf16[2,5760,32]{1,2,0:T(8,128)(2,1)} %param.6) | copy-start | bytes 2211844

commit v2 on v1

v2 whole, which is shorter than its diff:
```python
import functools

import jax
import jax.numpy as jnp
from jax import lax
from jax.experimental import pallas as pl
from jax.experimental.pallas import tpu as pltpu
from jax.sharding import PartitionSpec as P

NFREQ = 12
STEP = 3
MESH = pl.DeviceIdType.MESH
LANE = 128
TA1, TA2, TB1, TB2 = 14, 14, 9, 8
GROUP = (0, 64, 128, 256, 384, 448)
QUARTER = (16, 16, 32, 32, 16, 16)
NG = len(GROUP)
BOTH = (5,)


def pair_factor(valence_band, cond_band, valence_energy, cond_energy):
    nblk = valence_band.shape[0]
    nval = valence_energy.shape[0]
    ncon = cond_energy.shape[0]
    val_hot = valence_band[:, :, None] == jnp.arange(nval, dtype=jnp.int32)[None, None, :]
    con_hot = cond_band[:, :, None] == jnp.arange(ncon, dtype=jnp.int32)[None, None, :]
    low = jnp.sum(jnp.where(val_hot, valence_energy[None, None, :], 0.0), axis=2)
    high = jnp.sum(jnp.where(con_hot, cond_energy[None, None, :], 0.0), axis=2)
    low = low.reshape(nblk, 8, 2, 4).transpose(2, 1, 0, 3)
    delta = (high[None, None, :, None, :] - low[:, :, :, :, None]).reshape(1, -1)
    omega = 1.5 * jnp.arange(NFREQ).astype(jnp.float32)
    scale = 1.0 / jnp.sqrt(jnp.float32(delta.shape[1]))
    return -4.0 * delta / (delta**2 + omega[:, None] ** 2) * scale


def project_kernel(p_hbm, e_hbm, rows_out, cols_out, pairs, eig, total, landed, mid, mid_landed, halves, spread,
                   gather_send, gather_recv, copy_sem, eig_send, eig_recv, x_send, x_recv, y_send, y_recv,
                   spread_send, spread_recv, cols_send, cols_recv, rows_send, rows_recv, twin_send, twin_recv, local_sem):
    row, col = lax.axis_index("row"), lax.axis_index("col")
    core = lax.rem(col, 2)
    j = col // 2
    z, h = j // 2, lax.rem(j, 2)
    ylo, x = row // 4, lax.rem(row, 4)
    m_half = e_hbm.shape[0]
    source, mark = z // 2 == ylo, lax.rem(j, 4)
    place = lax.rem(z + 4 - 2 * ylo, 4)

    def seat(zz, hh, cc):
        return (row, zz * 4 + hh * 2 + cc)

    up = seat(lax.rem(z + 1, 4), h, core)
    down = seat(lax.rem(z + 3, 4), h, core)
    across = seat(z, 1 - h, core)
    twin = (row, col + 1 - 2 * core)

    block_rows = p_hbm.shape[1]
    local = [
        pltpu.make_async_copy(p_hbm.at[b], pairs.at[pl.ds(b * block_rows, block_rows)], copy_sem.at[b])
        for b in range(2)
    ]
    mine = pl.ds(pl.multiple_of(core * m_half, 16), m_half)
    local.append(pltpu.make_async_copy(e_hbm, eig.at[mine], copy_sem.at[2]))
    for c in local:
        c.start()

    barrier = pltpu.get_barrier_semaphore()

    def greet_rows(d, carry):
        other = ylo * 4 + lax.rem(x + d, 4)
        for c in range(2):
            pl.semaphore_signal(barrier, inc=1, device_id=(other, j * 2 + c), device_id_type=MESH)
        return carry

    def greet_cols(d, carry):
        other = lax.rem(j + d, 8)
        pl.semaphore_signal(barrier, inc=1, device_id=(row, other * 2 + core), device_id_type=MESH)
        return carry

    lax.fori_loop(1, 4, greet_rows, 0)
    lax.fori_loop(1, 8, greet_cols, 0)
    for other in (twin, ((1 - ylo) * 4 + x, col)):
        pl.semaphore_signal(barrier, inc=1, device_id=other, device_id_type=MESH)
    pl.semaphore_wait(barrier, 15)

    eig_copy = pltpu.make_async_remote_copy(
        e_hbm, eig.at[mine], eig_send, eig_recv, device_id=twin, device_id_type=MESH
    )

    a0, a1, a2 = 0, TA1 * LANE, (TA1 + TA2) * LANE
    b1, b2 = a2 + TB1 * LANE, a2 + (TB1 + TB2) * LANE
    piece = {"A": (a0, a2), "A1": (a0, a1), "A2": (a1, a2), "B": (a2, b2), "B1": (a2, b1), "B2": (b1, b2)}
    for name in ("A1", "A2"):
        lo, hi = piece[name]
        cut = lo + (hi - lo) // (2 * LANE) * LANE
        piece[name + "a"], piece[name + "b"] = (lo, cut), (cut, hi)

    slot_of = {(0, 0): 0, (0, 1): 1, (1, 0): 2, (3, 0): 3, (1, 1): 4, (3, 1): 5, (2, 0): 6, (2, 1): 7}
    place_of = {s: k for k, s in slot_of.items()}
    copies = {}
    begun = set()

    def region(slot, name):
        lo, hi = piece[name]
        return pairs.at[pl.ds(64 * slot, 64), pl.ds(lo, hi - lo)]

    def send(slot, name, way):
        dz, dh = place_of[slot]
        target, there = {
            "up": (up, ((dz + 3) % 4, dh)),
            "down": (down, ((dz + 1) % 4, dh)),
            "across": (across, (dz, 1 - dh)),
        }[way]
        there = slot_of[there]
        n = len(copies)
        c = pltpu.make_async_remote_copy(
            region(slot, name), region(there, name), gather_send.at[n], gather_recv.at[n],
            device_id=target, device_id_type=MESH,
        )
        copies[(there, name)] = c
        c.start()

    def arrive(slot, name):
        copies[(slot, name)].wait_recv()

    def multiply(first, last, name):
        lo, hi = piece[name]
        rows = pl.ds(64 * first, 64 * (last - first))
        value = lax.dot_general(
            pairs[rows, lo:hi], eig[:, lo:hi], (((1,), (1,)), ((), ())), preferred_element_type=jnp.float32
        )
        if first in begun:
            total[rows, :] += value
        else:
            total[rows, :] = value
        begun.update(range(first, last))

    def quarter(g):
        return pl.ds(sum(QUARTER[:g]), QUARTER[g])

    def pair_row(g, owner, jj, cc):
        if QUARTER[g] == 32:
            dz, dh, at = 1 + 2 * (owner // 2), g - 2, 32 * lax.rem(owner, 2)
        else:
            dz, dh, at = 2 * (g // 4), g % 2 if g < 2 else g - 4, 16 * owner
        zz = lax.rem(jj // 2 + dz, 4)
        hh = lax.rem(lax.rem(jj, 2) + dh, 2)
        return pl.multiple_of(cc * 512 + (zz * 2 + hh) * 64 + at, 16)

    def at_x(xx, cc):
        return (ylo * 4 + xx, j * 2 + cc)

    def own_rows(g, xx):
        return pl.ds(pl.multiple_of(GROUP[g] + xx * QUARTER[g], 16), QUARTER[g])

    def around(step):
        for d in (2, 1, 3):
            step(d, 0)

    def sum_x(g):
        def go(d, carry):
            to = lax.rem(x + d, 4)
            pltpu.make_async_remote_copy(
                total.at[own_rows(g, to)], landed.at[d - 1, quarter(g)], x_send.at[g], x_recv.at[g],
                device_id=at_x(to, core), device_id_type=MESH,
            ).start()
            return carry

        around(go)

    def y_copy(g):
        return pltpu.make_async_remote_copy(
            mid.at[quarter(g)], mid_landed.at[quarter(g)], y_send.at[g], y_recv.at[g],
            device_id=((1 - ylo) * 4 + x, col), device_id_type=MESH,
        )

    def sum_y(g):
        three = landed.at[:, quarter(g)]
        pltpu.make_async_copy(three, three, x_recv.at[g]).wait()
        value = total[own_rows(g, x), :]
        for d in range(3):
            value = value + landed[d, quarter(g), :]
        mid[quarter(g), :] = value
        y_copy(g).start()

    def spread_copy(g, k, zz, hh):
        block = spread.at[k, quarter(g)]
        return pltpu.make_async_remote_copy(
            block, block, spread_send, spread_recv.at[g, k], device_id=seat(zz, hh, core), device_id_type=MESH
        )

    def hand_rows(g):
        y_copy(g).wait_recv()
        value = (mid[quarter(g), :] + mid_landed[quarter(g), :]).astype(spread.dtype)

        @pl.when(source)
        def _():
            spread[mark, quarter(g), :] = value
            if g == NG - 1:
                spread_copy(g, mark, lax.rem(z + 2, 4), 1 - h).start()
                spread_copy(g, mark, lax.rem(z + 2, 4), h).start()
            for dz in (1, 3):
                spread_copy(g, mark, lax.rem(z + dz, 4), h).start()
            for dz in (1, 3):
                spread_copy(g, mark, lax.rem(z + dz, 4), 1 - h).start()
            spread_copy(g, mark, z, 1 - h).start()

        halves[0, quarter(g), :] = value[:, :m_half]
        halves[1, quarter(g), :] = value[:, m_half:]

    def spread_wait(g, k):
        block = spread.at[k, quarter(g)]
        pltpu.make_async_copy(block, block, spread_recv.at[g, k]).wait()

    def pass_z(g):
        @pl.when(place == 2)
        def _():
            for k in (2, 3):
                spread_wait(g, k)
                spread_copy(g, k, lax.rem(z + 1, 4), h).start()

        @pl.when(place == 3)
        def _():
            for k in (0, 1):
                spread_wait(g, k)
                spread_copy(g, k, lax.rem(z + 3, 4), h).start()

    def hand_cols(g):
        here = cols_out.at[pl.ds(pair_row(g, x, j, core), QUARTER[g])]

        def go_cols(d, carry):
            to = lax.rem(x + d, 4)
            for c in range(2):
                pltpu.make_async_remote_copy(
                    halves.at[c, quarter(g)], here, cols_send, cols_recv,
                    device_id=at_x(to, c), device_id_type=MESH,
                ).start()
            return carry

        around(go_cols)
        pltpu.make_async_remote_copy(
            halves.at[1 - core, quarter(g)], here, cols_send, cols_recv, device_id=twin, device_id_type=MESH
        ).start()
        pltpu.make_async_copy(halves.at[core, quarter(g)], here, local_sem.at[g]).start()

    def deal(g):
        for k in range(4):
            if g == NG - 1:
                pl.when(4 * ylo + k != j)(functools.partial(spread_wait, g, k))
            else:
                pl.when((4 * ylo + k != j) & (place != 3 - k // 2))(
                    functools.partial(spread_wait, g, k)
                )

        def there(to):
            return rows_out.at[pl.ds(pair_row(g, x, 4 * ylo + to, core), QUARTER[g])]

        def go(d, carry):
            to = lax.rem(x + d, 4)
            pltpu.make_async_remote_copy(
                spread.at[to, quarter(g)], there(to), rows_send, rows_recv.at[g],
                device_id=at_x(to, core), device_id_type=MESH,
            ).start()
            if g in BOTH:
                pltpu.make_async_remote_copy(
                    spread.at[to, quarter(g)], there(to), twin_send, twin_recv,
                    device_id=at_x(to, 1 - core), device_id_type=MESH,
                ).start()
            return carry

        around(go)
        kept = spread.at[x, quarter(g)]
        pltpu.make_async_copy(kept, there(x), local_sem.at[NG + g]).start()
        pltpu.make_async_remote_copy(
            kept, there(x), twin_send, twin_recv, device_id=twin, device_id_type=MESH
        ).start()

    def arrived(g):
        three = rows_out.at[pl.ds(0, 3 * QUARTER[g])]
        pltpu.make_async_copy(three, three, rows_recv.at[g]).wait()

    def pass_on(g):
        arrived(g)

        def go(d, carry):
            block = rows_out.at[pl.ds(pair_row(g, lax.rem(x + d, 4), row, core), QUARTER[g])]
            pltpu.make_async_remote_copy(
                block, block, twin_send, twin_recv, device_id=twin, device_id_type=MESH
            ).start()
            return carry

        around(go)

    local[0].wait()
    local[1].wait()
    send(0, "B", "up")
    send(0, "B", "down")
    send(0, "A", "across")
    eig_copy.start()
    send(0, "A", "up")
    send(0, "A", "down")
    send(0, "B", "across")
    local[2].wait()
    eig_copy.wait()
    multiply(0, 1, "B")
    multiply(0, 1, "A")
    sum_x(0)
    arrive(3, "B")
    send(3, "B1", "up")
    arrive(2, "B")
    send(2, "B2", "down")
    sum_y(0)
    send(3, "B", "across")
    send(2, "B", "across")
    arrive(1, "A")
    send(1, "A", "up")
    send(1, "A", "down")
    arrive(3, "A")
    send(3, "A1", "up")
    arrive(2, "A")
    send(2, "A2", "down")
    multiply(1, 4, "A")
    arrive(1, "B")
    multiply(1, 4, "B")
    sum_x(1)
    sum_x(2)
    arrive(6, "B1")
    arrive(6, "B2")
    multiply(6, 7, "B")
    sum_y(1)
    sum_y(2)
    send(6, "B1", "across")
    send(6, "B2", "across")
    arrive(5, "A")
    send(5, "A1a", "up")
    send(5, "A1b", "up")
    arrive(4, "A")
    send(4, "A2a", "down")
    send(4, "A2b", "down")
    hand_rows(0)
    hand_cols(0)
    arrive(5, "B")
    arrive(4, "B")
    multiply(4, 6, "B")
    multiply(4, 6, "A")
    sum_x(3)
    hand_rows(1)
    hand_rows(2)
    hand_cols(1)
    hand_cols(2)
    arrive(6, "A1")
    arrive(6, "A2")
    multiply(6, 7, "A")
    sum_x(4)
    arrive(7, "A1a")
    multiply(7, 8, "A1a")
    arrive(7, "A2a")
    multiply(7, 8, "A2a")
    arrive(7, "B1")
    arrive(7, "B2")
    multiply(7, 8, "B")
    arrive(7, "A1b")
    multiply(7, 8, "A1b")
    arrive(7, "A2b")
    multiply(7, 8, "A2b")
    sum_x(5)
    sum_y(3)
    sum_y(4)
    pass_z(0)
    pass_z(1)
    pass_z(2)
    hand_rows(3)
    sum_y(5)
    hand_rows(4)
    hand_cols(3)
    hand_cols(4)
    deal(0)
    deal(1)
    deal(2)
    hand_rows(5)
    hand_cols(5)
    pass_z(3)
    pass_z(4)
    deal(3)
    deal(4)
    pass_on(0)
    pass_on(1)
    pass_on(2)
    pass_on(3)
    pass_on(4)
    deal(5)
    arrived(5)

    for c in copies.values():
        c.wait_send()
    for g in range(NG):
        three = landed.at[:, quarter(g)]
        pltpu.make_async_copy(three, three, x_send.at[g]).wait()
        y_copy(g).wait_send()
        for n, block in ((g, cols_out.at[pl.ds(0, QUARTER[g])]), (NG + g, rows_out.at[pl.ds(0, QUARTER[g])])):
            pltpu.make_async_copy(block, block, local_sem.at[n]).wait()

    def wait_rows(ref, count, s):
        block = ref.at[pl.ds(0, count)]
        pltpu.make_async_copy(block, block, s).wait()

    mine = sum(QUARTER)

    @pl.when(source)
    def _():
        wait_rows(rows_out, 5 * mine + 2 * QUARTER[NG - 1], spread_send)

    @pl.when(place >= 2)
    def _():
        wait_rows(rows_out, 2 * (mine - QUARTER[NG - 1]), spread_send)

    wait_rows(cols_out, 7 * mine, cols_send)
    wait_rows(cols_out, 7 * mine, cols_recv)
    wait_rows(rows_out, 3 * mine, rows_send)
    wait_rows(rows_out, 4 * mine, twin_send)
    wait_rows(rows_out, 4 * mine, twin_recv)


def project(pairs_t, eig_t):
    nblk, pair_rows, depth = pairs_t.shape
    m_half = eig_t.shape[0]
    m_all = 2 * m_half
    bf16, f32 = jnp.bfloat16, jnp.float32
    dma = pltpu.SemaphoreType.DMA
    mine = sum(QUARTER)
    return pl.pallas_call(
        project_kernel,
        out_shape=(
            jax.ShapeDtypeStruct((1024, m_all), bf16),
            jax.ShapeDtypeStruct((1024, m_half), bf16),
        ),
        in_specs=[pl.BlockSpec(memory_space=pltpu.HBM)] * 2,
        out_specs=(pl.BlockSpec(memory_space=pl.ANY),) * 2,
        scratch_shapes=[
            pltpu.VMEM((512, depth), bf16),
            pltpu.VMEM((m_all, depth), bf16),
            pltpu.VMEM((512, m_all), f32),
            pltpu.VMEM((3, mine, m_all), f32),
            pltpu.VMEM((mine, m_all), f32),
            pltpu.VMEM((mine, m_all), f32),
            pltpu.VMEM((2, mine, m_half), bf16),
            pltpu.VMEM((4, mine, m_all), bf16),
            dma((20,)), dma((20,)), dma((3,)), dma, dma, dma((NG,)), dma((NG,)), dma((NG,)), dma((NG,)),
            dma, dma((NG, 4)), dma, dma, dma, dma((NG,)), dma, dma, dma((2 * NG,)),
        ],
        compiler_params=pltpu.CompilerParams(
            collective_id=0, has_side_effects=True, vmem_limit_bytes=48 * 2**20
        ),
        name="project",
    )(*(pltpu.with_memory_space_constraint(a, pltpu.HBM) for a in (pairs_t, eig_t)))


def chi_kernel(factor_ref, rows_ref, cols_ref, out_ref, cols_t, scaled):
    @pl.when(pl.program_id(0) == 0)
    def _():
        cols_t[...] = cols_ref[...].astype(jnp.float32).T

    s_cols = cols_t.shape[0]
    for w in range(STEP):
        scaled[w * s_cols:(w + 1) * s_cols] = (
            cols_t[...] * factor_ref[pl.ds(pl.program_id(0) * STEP + w, 1), :]
        ).astype(scaled.dtype)
    value = jnp.dot(scaled[...], rows_ref[...], preferred_element_type=jnp.float32)
    out_ref[...] = value.reshape(out_ref.shape)


def polarizability(factor, rows, cols):
    n, s_rows = rows.shape
    s_cols = cols.shape[1]
    return pl.pallas_call(
        chi_kernel,
        grid=(NFREQ // STEP,),
        out_shape=jax.ShapeDtypeStruct((NFREQ, s_cols, s_rows), jnp.float32),
        in_specs=[
            pl.BlockSpec((NFREQ, n), lambda w: (0, 0)),
            pl.BlockSpec((n, s_rows), lambda w: (0, 0)),
            pl.BlockSpec((n, s_cols), lambda w: (0, 0)),
        ],
        out_specs=pl.BlockSpec((STEP, s_cols, s_rows), lambda w: (w, 0, 0)),
        scratch_shapes=[pltpu.VMEM((s_cols, n), jnp.float32), pltpu.VMEM((STEP * s_cols, n), jnp.bfloat16)],
        compiler_params=pltpu.CompilerParams(vmem_limit_bytes=32 * 2**20),
        name="chi",
    )(factor, rows, cols)


def local(pair_products, eigvecs, valence_band, cond_band, valence_energy, cond_energy):
    factor = pair_factor(valence_band, cond_band, valence_energy, cond_energy)
    rows, cols = project(pair_products.transpose(0, 2, 1), eigvecs.T)
    return polarizability(factor, rows, cols).transpose(0, 2, 1)


def solution(mesh):
    return jax.shard_map(
        local,
        mesh=mesh,
        in_specs=(P(None, "row", "col"), P("row", "col"), P(), P(), P(), P()),
        out_specs=P(None, "row", "col"),
        check_vma=False,
    )
```

time: 113 us -> 83.2 us (0.74); the launches traced: 111 us -> 82.9 us
  Pallas kernels: 105 us -> 80.2 us
  local copies, waits for them, and re-layouts: 3.37 us -> 0.32 us
    pallas_call x1, Pallas kernels: 95.2 us -> 72.4 us  [project(): pl.pallas_call(project_kernel, out_shape=(jax.ShapeDtypeStruct((1024, m_a...]
    unnamed x4 -> x0, local copies, waits for them, and re-layouts: 3.05 us -> none
    pallas_call x1, Pallas kernels: 10 us -> 7.86 us  [polarizability(): pl.pallas_call(chi_kernel, grid=(NFREQ // STEP,), out_shape=jax.ShapeDtyp...]
where the time goes in v2:
time: 83.2 us; the launch traced here: 82.9 us
  Pallas kernels  80.2 us (96%)
  other arithmetic  2.37 us (3%)
    pallas_call x1, Pallas kernels, project(): pl.pallas_call(project_kernel, out_shape=(jax.ShapeDtypeStruct((1024, m_a...  72.4 us
    pallas_call x1, Pallas kernels, polarizability(): pl.pallas_call(chi_kernel, grid=(NFREQ // STEP,), out_shape=jax.ShapeDtyp...  7.86 us

profile of v2, /device:TPU:9, one launch (start us, length us, event | category | flops | bytes accessed | tf_op | source)
XLA Modules:
  0.0 82.9 jit_solution(12047413380540671737)
XLA Ops:
  0.0 1.3 %select_reduce_fusion = f32[2,64]{1,0:T(2,128)S(1)} fusion(f32[5484]{0:T(1024)} %param.10, s32[2,64]{1,0:T(2,128)} %param.8), kind=kLoop, calls=%fused_computation | loop fusion | flops 2105728 | bytes 22960 | tf_op jit(solution)/shard_map/reduce_sum | solution.py:27
  1.3 0.9 %select_reduce_fusion.1 = f32[2,8]{1,0:T(2,128)S(1)} fusion(f32[4096]{0:T(1024)} %param.11, s32[2,8]{1,0:T(2,128)} %param.9), kind=kLoop, calls=%fused_computation.2 | loop fusion | flops 196592 | bytes 16512 | tf_op jit(solution)/shard_map/reduce_sum | solution.py:28
  2.2 0.1 reshape.46
  2.3 0.1 subtract_multiply_fusion.1
  2.4 0.1 mul.29
  2.5 0.1 integer_pow.20
  2.6 0.1 divide_multiply_fusion.factor_ref
  2.7 72.4 %project.1 = (bf16[1024,576]{1,0:T(8,128)(2,1)S(1)}, bf16[1024,288]{1,0:T(8,128)(2,1)S(1)}) custom-call(bf16[2,32,5760]{2,1,0:T(8,128)(2,1)} %bitcast.5, bf16[288,5760]{1,0:T(8,128)(2,1)} %bitcast.4), custom_call_target="tpu_custom_call" | custom-call | tf_op jit(solution)/shard_map/project/pallas_call | solution.py:430
  75.1 7.9 %chi.1 = f32[12,288,576]{2,1,0:T(8,128)} custom-call(f32[12,1024]{1,0:T(8,128)S(1)} %divide_multiply_fusion.factor_ref, bf16[1024,576]{1,0:T(8,128)(2,1)S(1)} %get-tuple-element.7.rows_ref, bf16[1024,288]{1,0:T(8,128)(2,1)S(1)} %get-tuple-element.8.cols_ref), custom_call_target="tpu_custom_call" | custom-call | tf_op jit(solution)/shard_map/chi/pallas_call | solution.py:474
  (2 shorter events, 0.0 us)

commit v3 on v2

--- a/solution.py
+++ b/solution.py
@@ -15,27 +15,15 @@
 GROUP = (0, 64, 128, 256, 384, 448)
 QUARTER = (16, 16, 32, 32, 16, 16)
 NG = len(GROUP)
-BOTH = (5,)
-
-
-def pair_factor(valence_band, cond_band, valence_energy, cond_energy):
-    nblk = valence_band.shape[0]
-    nval = valence_energy.shape[0]
-    ncon = cond_energy.shape[0]
-    val_hot = valence_band[:, :, None] == jnp.arange(nval, dtype=jnp.int32)[None, None, :]
-    con_hot = cond_band[:, :, None] == jnp.arange(ncon, dtype=jnp.int32)[None, None, :]
-    low = jnp.sum(jnp.where(val_hot, valence_energy[None, None, :], 0.0), axis=2)
-    high = jnp.sum(jnp.where(con_hot, cond_energy[None, None, :], 0.0), axis=2)
-    low = low.reshape(nblk, 8, 2, 4).transpose(2, 1, 0, 3)
-    delta = (high[None, None, :, None, :] - low[:, :, :, :, None]).reshape(1, -1)
-    omega = 1.5 * jnp.arange(NFREQ).astype(jnp.float32)
-    scale = 1.0 / jnp.sqrt(jnp.float32(delta.shape[1]))
-    return -4.0 * delta / (delta**2 + omega[:, None] ** 2) * scale
-
-
-def project_kernel(p_hbm, e_hbm, rows_out, cols_out, pairs, eig, total, landed, mid, mid_landed, halves, spread,
+FAR = (3, 4, 5)
+BOTH = (3, 4, 5)
+
+
+def project_kernel(p_hbm, e_hbm, vband_hbm, cband_hbm, venergy_hbm, cenergy_hbm, rows_out, cols_out, factor_out,
+                   pairs, eig, total, landed, mid, mid_landed, halves, spread,
                    gather_send, gather_recv, copy_sem, eig_send, eig_recv, x_send, x_recv, y_send, y_recv,
-                   spread_send, spread_recv, cols_send, cols_recv, rows_send, rows_recv, twin_send, twin_recv, local_sem):
+                   spread_send, spread_recv, cols_send, cols_recv, rows_send, rows_recv, twin_send, twin_recv, local_sem,
+                   vband, cband, venergy, cenergy, factors, table_sem, factor_sem):
     row, col = lax.axis_index("row"), lax.axis_index("col")
     core = lax.rem(col, 2)
     j = col // 2
@@ -61,6 +49,15 @@
     mine = pl.ds(pl.multiple_of(core * m_half, 16), m_half)
     local.append(pltpu.make_async_copy(e_hbm, eig.at[mine], copy_sem.at[2]))
     for c in local:
+        c.start()
+
+    tables = [
+        pltpu.make_async_copy(src, dst, table_sem.at[n])
+        for n, (src, dst) in enumerate(
+            ((vband_hbm, vband), (cband_hbm, cband), (venergy_hbm, venergy), (cenergy_hbm, cenergy))
+        )
+    ]
+    for c in tables:
         c.start()
 
     barrier = pltpu.get_barrier_semaphore()
@@ -152,6 +149,36 @@
     def own_rows(g, xx):
         return pl.ds(pl.multiple_of(GROUP[g] + xx * QUARTER[g], 16), QUARTER[g])
 
+    def pair_factors():
+        for c in tables:
+            c.wait()
+        nblk, nv = vband.shape
+        nc = cband.shape[1]
+        part_of = lax.broadcasted_iota(jnp.int32, (8, LANE), 0)
+        lane = lax.broadcasted_iota(jnp.int32, (8, LANE), 1)
+        blk = (lane // 32) % 2
+        v_of = blk * nv + ((part_of % 4) * 2 + lane // 64) * 8 + (part_of // 4) * 4 + (lane % 32) // 8
+        c_of = blk * nc + lane % 8
+
+        def valence(i, low):
+            for n in range(4):
+                i4 = i * 4 + n
+                low = jnp.where(v_of == i4, venergy[vband[i4 // nv, i4 % nv]], low)
+            return low
+
+        def conduction(i, high):
+            return jnp.where(c_of == i, cenergy[cband[i // nc, i % nc]], high)
+
+        low = lax.fori_loop(0, nblk * nv // 4, valence, jnp.zeros((8, LANE), jnp.float32))
+        high = lax.fori_loop(0, nblk * nc, conduction, jnp.zeros((8, LANE), jnp.float32))
+        delta = high - low
+        scale = 1.0 / (8 * LANE) ** 0.5
+        for w in range(NFREQ):
+            value = -4.0 * delta / (delta * delta + (1.5 * w) ** 2) * scale
+            for n in range(8):
+                factors[w:w + 1, n * LANE:(n + 1) * LANE] = value[n:n + 1, :]
+        pltpu.make_async_copy(factors, factor_out, factor_sem).start()
+
     def around(step):
         for d in (2, 1, 3):
             step(d, 0)
@@ -195,7 +222,7 @@
         @pl.when(source)
         def _():
             spread[mark, quarter(g), :] = value
-            if g == NG - 1:
+            if g in FAR:
                 spread_copy(g, mark, lax.rem(z + 2, 4), 1 - h).start()
                 spread_copy(g, mark, lax.rem(z + 2, 4), h).start()
             for dz in (1, 3):
@@ -244,7 +271,7 @@
 
     def deal(g):
         for k in range(4):
-            if g == NG - 1:
+            if g in FAR:
                 pl.when(4 * ylo + k != j)(functools.partial(spread_wait, g, k))
             else:
                 pl.when((4 * ylo + k != j) & (place != 3 - k // 2))(
@@ -299,6 +326,7 @@
     send(0, "A", "up")
     send(0, "A", "down")
     send(0, "B", "across")
+    pair_factors()
     local[2].wait()
     eig_copy.wait()
     multiply(0, 1, "B")
@@ -378,18 +406,17 @@
     deal(2)
     hand_rows(5)
     hand_cols(5)
-    pass_z(3)
-    pass_z(4)
     deal(3)
     deal(4)
+    deal(5)
     pass_on(0)
     pass_on(1)
     pass_on(2)
-    pass_on(3)
-    pass_on(4)
-    deal(5)
+    arrived(3)
+    arrived(4)
     arrived(5)
 
+    pltpu.make_async_copy(factors, factor_out, factor_sem).wait()
     for c in copies.values():
         c.wait_send()
     for g in range(NG):
@@ -403,15 +430,15 @@
         block = ref.at[pl.ds(0, count)]
         pltpu.make_async_copy(block, block, s).wait()
 
-    mine = sum(QUARTER)
+    mine, far = sum(QUARTER), sum(QUARTER[g] for g in FAR)
 
     @pl.when(source)
     def _():
-        wait_rows(rows_out, 5 * mine + 2 * QUARTER[NG - 1], spread_send)
+        wait_rows(rows_out, 5 * mine + 2 * far, spread_send)
 
     @pl.when(place >= 2)
     def _():
-        wait_rows(rows_out, 2 * (mine - QUARTER[NG - 1]), spread_send)
+        wait_rows(rows_out, 2 * (mine - far), spread_send)
 
     wait_rows(cols_out, 7 * mine, cols_send)
     wait_rows(cols_out, 7 * mine, cols_recv)
@@ -420,7 +447,7 @@
     wait_rows(rows_out, 4 * mine, twin_recv)
 
 
-def project(pairs_t, eig_t):
+def project(pairs_t, eig_t, *tables):
     nblk, pair_rows, depth = pairs_t.shape
     m_half = eig_t.shape[0]
     m_all = 2 * m_half
@@ -432,9 +459,10 @@
         out_shape=(
             jax.ShapeDtypeStruct((1024, m_all), bf16),
             jax.ShapeDtypeStruct((1024, m_half), bf16),
+            jax.ShapeDtypeStruct((NFREQ, 1024), f32),
         ),
-        in_specs=[pl.BlockSpec(memory_space=pltpu.HBM)] * 2,
-        out_specs=(pl.BlockSpec(memory_space=pl.ANY),) * 2,
+        in_specs=[pl.BlockSpec(memory_space=pltpu.HBM)] * 6,
+        out_specs=(pl.BlockSpec(memory_space=pl.ANY),) * 3,
         scratch_shapes=[
             pltpu.VMEM((512, depth), bf16),
             pltpu.VMEM((m_all, depth), bf16),
@@ -446,23 +474,24 @@
             pltpu.VMEM((4, mine, m_all), bf16),
             dma((20,)), dma((20,)), dma((3,)), dma, dma, dma((NG,)), dma((NG,)), dma((NG,)), dma((NG,)),
             dma, dma((NG, 4)), dma, dma, dma, dma((NG,)), dma, dma, dma((2 * NG,)),
+            *(pltpu.SMEM(a.shape, a.dtype) for a in tables), pltpu.VMEM((NFREQ, 1024), f32), dma((4,)), dma,
         ],
         compiler_params=pltpu.CompilerParams(
             collective_id=0, has_side_effects=True, vmem_limit_bytes=48 * 2**20
         ),
         name="project",
-    )(*(pltpu.with_memory_space_constraint(a, pltpu.HBM) for a in (pairs_t, eig_t)))
+    )(*(pltpu.with_memory_space_constraint(a, pltpu.HBM) for a in (pairs_t, eig_t, *tables)))
 
 
 def chi_kernel(factor_ref, rows_ref, cols_ref, out_ref, cols_t, scaled):
     @pl.when(pl.program_id(0) == 0)
     def _():
-        cols_t[...] = cols_ref[...].astype(jnp.float32).T
+        cols_t[...] = cols_ref[...].T
 
     s_cols = cols_t.shape[0]
     for w in range(STEP):
         scaled[w * s_cols:(w + 1) * s_cols] = (
-            cols_t[...] * factor_ref[pl.ds(pl.program_id(0) * STEP + w, 1), :]
+            cols_t[...].astype(jnp.float32) * factor_ref[pl.ds(pl.program_id(0) * STEP + w, 1), :]
         ).astype(scaled.dtype)
     value = jnp.dot(scaled[...], rows_ref[...], preferred_element_type=jnp.float32)
     out_ref[...] = value.reshape(out_ref.shape)
@@ -475,21 +504,18 @@
         chi_kernel,
         grid=(NFREQ // STEP,),
         out_shape=jax.ShapeDtypeStruct((NFREQ, s_cols, s_rows), jnp.float32),
-        in_specs=[
-            pl.BlockSpec((NFREQ, n), lambda w: (0, 0)),
-            pl.BlockSpec((n, s_rows), lambda w: (0, 0)),
-            pl.BlockSpec((n, s_cols), lambda w: (0, 0)),
-        ],
+        in_specs=[pl.BlockSpec(memory_space=pltpu.VMEM)] * 3,
         out_specs=pl.BlockSpec((STEP, s_cols, s_rows), lambda w: (w, 0, 0)),
-        scratch_shapes=[pltpu.VMEM((s_cols, n), jnp.float32), pltpu.VMEM((STEP * s_cols, n), jnp.bfloat16)],
+        scratch_shapes=[pltpu.VMEM((s_cols, n), jnp.bfloat16), pltpu.VMEM((STEP * s_cols, n), jnp.bfloat16)],
         compiler_params=pltpu.CompilerParams(vmem_limit_bytes=32 * 2**20),
         name="chi",
     )(factor, rows, cols)
 
 
 def local(pair_products, eigvecs, valence_band, cond_band, valence_energy, cond_energy):
-    factor = pair_factor(valence_band, cond_band, valence_energy, cond_energy)
-    rows, cols = project(pair_products.transpose(0, 2, 1), eigvecs.T)
+    rows, cols, factor = project(
+        pair_products.transpose(0, 2, 1), eigvecs.T, valence_band, cond_band, valence_energy, cond_energy
+    )
     return polarizability(factor, rows, cols).transpose(0, 2, 1)
 
 

time: 83.2 us -> 79.1 us (0.951)
  other arithmetic: 2.37 us -> 0 us
  Pallas kernels: 80.2 us -> 79 us
    reduce_sum x2 -> x0, other arithmetic: 2.17 us -> none  [the longest x1 1.26 us: pair_factor(): jnp.sum(jnp.where(val_hot, valence_energy[None, None, :], 0.0), axis=2)]
    pallas_call x1, Pallas kernels: 72.4 us -> 71.2 us  [project(): pl.pallas_call(project_kernel, out_shape=(jax.ShapeDtypeStruct((1024, m_a...]
where the time goes in v3:
time: 79.1 us; the launch traced here: 79 us
  Pallas kernels  79 us (100%)
    pallas_call x1, Pallas kernels, project(): pl.pallas_call(project_kernel, out_shape=(jax.ShapeDtypeStruct((1024, m_a...  71.2 us
    pallas_call x1, Pallas kernels, polarizability(): pl.pallas_call(chi_kernel, grid=(NFREQ // STEP,), out_shape=jax.ShapeDtyp...  7.84 us

profile of v3, /device:TPU:9, one launch (start us, length us, event | category | flops | bytes accessed | tf_op | source)
XLA Modules:
  0.0 79.0 jit_solution(9033871018346075464)
XLA Ops:
  0.0 71.2 %project.1 = (bf16[1024,576]{1,0:T(8,128)(2,1)S(1)}, bf16[1024,288]{1,0:T(8,128)(2,1)S(1)}, f32[12,1024]{1,0:T(8,128)S(1)}) custom-call(bf16[2,32,5760]{2,1,0:T(8,128)(2,1)} %bitcast.4, bf16[288,5760]{1,0:T(8,128)(2,1)} %bitcast.3, s32[2,64]{1,0:T(2,128)} %vband_hbm.1, s32[2,8]{1,0:T(2,128)} %cband_hbm.1, f32[5484]{0:T(1024)} %venergy_hbm.1, f32[4096]{0:T(1024)} %cenergy_hbm.1), custom_call_target="tpu_custom_call" | custom-call | tf_op jit(solution)/shard_map/project/pallas_call | solution.py:457
  71.2 7.8 %chi.1 = f32[12,288,576]{2,1,0:T(8,128)} custom-call(f32[12,1024]{1,0:T(8,128)S(1)} %get-tuple-element.8.factor_ref, bf16[1024,576]{1,0:T(8,128)(2,1)S(1)} %get-tuple-element.9.rows_ref, bf16[1024,288]{1,0:T(8,128)(2,1)S(1)} %get-tuple-element.10.cols_ref), custom_call_target="tpu_custom_call" | custom-call | tf_op jit(solution)/shard_map/chi/pallas_call | solution.py:503

commit v4 on v3

--- a/solution.py
+++ b/solution.py
@@ -16,7 +16,7 @@
 QUARTER = (16, 16, 32, 32, 16, 16)
 NG = len(GROUP)
 FAR = (3, 4, 5)
-BOTH = (3, 4, 5)
+BOTH = (5,)
 
 
 def project_kernel(p_hbm, e_hbm, vband_hbm, cband_hbm, venergy_hbm, cenergy_hbm, rows_out, cols_out, factor_out,
@@ -369,12 +369,12 @@
     arrive(5, "B")
     arrive(4, "B")
     multiply(4, 6, "B")
-    multiply(4, 6, "A")
-    sum_x(3)
     hand_rows(1)
     hand_rows(2)
     hand_cols(1)
     hand_cols(2)
+    multiply(4, 6, "A")
+    sum_x(3)
     arrive(6, "A1")
     arrive(6, "A2")
     multiply(6, 7, "A")
@@ -408,12 +408,12 @@
     hand_cols(5)
     deal(3)
     deal(4)
-    deal(5)
     pass_on(0)
     pass_on(1)
     pass_on(2)
-    arrived(3)
-    arrived(4)
+    deal(5)
+    pass_on(3)
+    pass_on(4)
     arrived(5)
 
     pltpu.make_async_copy(factors, factor_out, factor_sem).wait()

time: 79.1 us -> 77.1 us (0.975)
  Pallas kernels: 79 us -> 77 us
    pallas_call x1, Pallas kernels: 71.2 us -> 69.1 us  [project(): pl.pallas_call(project_kernel, out_shape=(jax.ShapeDtypeStruct((1024, m_a...]
where the time goes in v4:
time: 77.1 us; the launch traced here: 77 us
  Pallas kernels  77 us (100%)
    pallas_call x1, Pallas kernels, project(): pl.pallas_call(project_kernel, out_shape=(jax.ShapeDtypeStruct((1024, m_a...  69.1 us
    pallas_call x1, Pallas kernels, polarizability(): pl.pallas_call(chi_kernel, grid=(NFREQ // STEP,), out_shape=jax.ShapeDtyp...  7.84 us

profile of v4, /device:TPU:9, one launch (start us, length us, event | category | flops | bytes accessed | tf_op | source)
XLA Modules:
  0.0 77.0 jit_solution(7537504735904022874)
XLA Ops:
  0.0 69.1 %project.1 = (bf16[1024,576]{1,0:T(8,128)(2,1)S(1)}, bf16[1024,288]{1,0:T(8,128)(2,1)S(1)}, f32[12,1024]{1,0:T(8,128)S(1)}) custom-call(bf16[2,32,5760]{2,1,0:T(8,128)(2,1)} %bitcast.4, bf16[288,5760]{1,0:T(8,128)(2,1)} %bitcast.3, s32[2,64]{1,0:T(2,128)} %vband_hbm.1, s32[2,8]{1,0:T(2,128)} %cband_hbm.1, f32[5484]{0:T(1024)} %venergy_hbm.1, f32[4096]{0:T(1024)} %cenergy_hbm.1), custom_call_target="tpu_custom_call" | custom-call | tf_op jit(solution)/shard_map/project/pallas_call | solution.py:457
  69.1 7.8 %chi.1 = f32[12,288,576]{2,1,0:T(8,128)} custom-call(f32[12,1024]{1,0:T(8,128)S(1)} %get-tuple-element.8.factor_ref, bf16[1024,576]{1,0:T(8,128)(2,1)S(1)} %get-tuple-element.9.rows_ref, bf16[1024,288]{1,0:T(8,128)(2,1)S(1)} %get-tuple-element.10.cols_ref), custom_call_target="tpu_custom_call" | custom-call | tf_op jit(solution)/shard_map/chi/pallas_call | solution.py:503

commit v5 on v4

--- a/solution.py
+++ b/solution.py
@@ -397,9 +397,9 @@
     pass_z(1)
     pass_z(2)
     hand_rows(3)
+    hand_cols(3)
     sum_y(5)
     hand_rows(4)
-    hand_cols(3)
     hand_cols(4)
     deal(0)
     deal(1)
@@ -407,9 +407,9 @@
     hand_rows(5)
     hand_cols(5)
     deal(3)
-    deal(4)
     pass_on(0)
     pass_on(1)
+    deal(4)
     pass_on(2)
     deal(5)
     pass_on(3)

time: 77.1 us -> 77 us (level)
  Pallas kernels: 77 us -> 76.1 us
    pallas_call x1, Pallas kernels: 69.1 us -> 68.3 us  [project(): pl.pallas_call(project_kernel, out_shape=(jax.ShapeDtypeStruct((1024, m_a...]
where the time goes in v5:
time: 77 us; the launch traced here: 76.1 us
  Pallas kernels  76.1 us (99%)
    pallas_call x1, Pallas kernels, project(): pl.pallas_call(project_kernel, out_shape=(jax.ShapeDtypeStruct((1024, m_a...  68.3 us
    pallas_call x1, Pallas kernels, polarizability(): pl.pallas_call(chi_kernel, grid=(NFREQ // STEP,), out_shape=jax.ShapeDtyp...  7.85 us

profile of v5, /device:TPU:9, one launch (start us, length us, event | category | flops | bytes accessed | tf_op | source)
XLA Modules:
  0.0 76.1 jit_solution(5578904841333012284)
XLA Ops:
  0.0 68.3 %project.1 = (bf16[1024,576]{1,0:T(8,128)(2,1)S(1)}, bf16[1024,288]{1,0:T(8,128)(2,1)S(1)}, f32[12,1024]{1,0:T(8,128)S(1)}) custom-call(bf16[2,32,5760]{2,1,0:T(8,128)(2,1)} %bitcast.4, bf16[288,5760]{1,0:T(8,128)(2,1)} %bitcast.3, s32[2,64]{1,0:T(2,128)} %vband_hbm.1, s32[2,8]{1,0:T(2,128)} %cband_hbm.1, f32[5484]{0:T(1024)} %venergy_hbm.1, f32[4096]{0:T(1024)} %cenergy_hbm.1), custom_call_target="tpu_custom_call" | custom-call | tf_op jit(solution)/shard_map/project/pallas_call | solution.py:457
  68.3 7.8 %chi.1 = f32[12,288,576]{2,1,0:T(8,128)} custom-call(f32[12,1024]{1,0:T(8,128)S(1)} %get-tuple-element.8.factor_ref, bf16[1024,576]{1,0:T(8,128)(2,1)S(1)} %get-tuple-element.9.rows_ref, bf16[1024,288]{1,0:T(8,128)(2,1)S(1)} %get-tuple-element.10.cols_ref), custom_call_target="tpu_custom_call" | custom-call | tf_op jit(solution)/shard_map/chi/pallas_call | solution.py:503
